TPU v7x, 512 devices: a whole 4x4x16 slice. The times are simulated.
512 devices in a mesh: blk: 8 (over z_lo, core), aux: 64 (over z_hi, x, y).
Axes of the slice: x: 4, y: 4, z: 16 (z_hi: 4, z_lo: 4; z = z_hi * 4 + z_lo), core: 2. Of those that a mesh axis runs over, the one named last changes fastest.
Arguments:
- three_index: bfloat16 [12800, 16, 4096], P('aux', 'blk'), may hold values from -1 to 1
- occ_energy: float32 [16], replicated, may hold values from -1.5 to -0.4
- vir_energy: float32 [4096], replicated, may hold values from 0.2 to 2.5
Outputs:
- vv_density: float32 [768, 96], P('blk')
- oo_density: float32 [16, 2], P('blk')
All inputs are finite; a program needn't handle non-finite values.
Results may differ from a plain program's by a relative error of at most 0.00055.
Values may be sent and summed in bfloat16 or wider, within the bound.
A program may use at most 64 MiB of HBM per device.

v0:
```python
import jax
import jax.numpy as jnp
from jax import lax
from jax.sharding import PartitionSpec as P

AW = 96


def shifted(x, axis, by):
    devices = lax.axis_size(axis)
    return lax.ppermute(x, axis, [(i, (i + by) % devices) for i in range(devices)])


def amplitude(kmat, row_energy, col_energy, win_energy, tile_energy):
    denom = (
        row_energy[:, None, None, None]
        + col_energy[None, None, :, None]
        - win_energy[None, :, None, None]
        - tile_energy[None, None, None, :]
    )
    return kmat / denom


def own_terms(t_own):
    tt_own = 2.0 * t_own - jnp.transpose(t_own, (2, 1, 0, 3))
    vv_part = jnp.einsum("iajb,icjb->ac", t_own, tt_own)
    oo_part = jnp.einsum("iakb,jakb->ij", t_own, tt_own)
    return (vv_part, oo_part)


def cross_terms(t_op, t_po):
    tt_op = 2.0 * t_op - jnp.transpose(t_po, (2, 1, 0, 3))
    tt_po = 2.0 * t_po - jnp.transpose(t_op, (2, 1, 0, 3))
    vv_part = jnp.einsum("iajb,icjb->ac", t_op, tt_op) + jnp.einsum("iajb,icjb->ac", t_po, tt_po)
    oo_part = jnp.einsum("iakb,jakb->ij", t_op, tt_op)
    return (vv_part, oo_part)


def contract(left, right):
    return lax.dot_general(
        left, right, (((0,), (0,)), ((), ())), preferred_element_type=jnp.float32
    )


def shards(three_index, occ_energy, vir_energy):
    aux_rows, occ_block, vir_count = three_index.shape
    aux_count = lax.axis_size("aux")
    blk_count = lax.axis_size("blk")
    tile_width = vir_count // aux_count
    block_index = lax.axis_index("blk")
    prev_index = (block_index + blk_count - 1) % blk_count
    aux_index = lax.axis_index("aux")
    e_own = lax.dynamic_slice_in_dim(occ_energy, block_index * occ_block, occ_block, 0)
    e_prev = lax.dynamic_slice_in_dim(occ_energy, prev_index * occ_block, occ_block, 0)
    win_energy = vir_energy[:AW]
    tile_energy = lax.dynamic_slice_in_dim(vir_energy, aux_index * tile_width, tile_width, 0)
    seq = jnp.arange(occ_block, dtype=jnp.int32)
    offdiag = (seq[:, None] != seq[None, :]).astype(jnp.float32)
    slab_local = three_index[:, :, :AW].reshape(aux_rows, occ_block * AW)
    tile_own = lax.all_to_all(three_index, "aux", split_axis=2, concat_axis=0, tiled=True).reshape(
        -1, occ_block * tile_width
    )
    shape_four = (occ_block, AW, occ_block, tile_width)
    slab_all = lax.all_gather(slab_local, "aux", axis=0, tiled=True)
    tile_prv, slab_prv = shifted((tile_own, slab_all), "blk", 1)
    ints_own = contract(slab_all, tile_own).reshape(shape_four)
    ints_op = contract(slab_all, tile_prv).reshape(shape_four)
    ints_po = contract(slab_prv, tile_own).reshape(shape_four)
    t_own = amplitude(ints_own, e_own, e_own, win_energy, tile_energy) * offdiag[:, None, :, None]
    t_op = amplitude(ints_op, e_own, e_prev, win_energy, tile_energy)
    t_po = amplitude(ints_po, e_prev, e_own, win_energy, tile_energy)
    vv_own, oo_own = own_terms(t_own)
    vv_cross, oo_cross = cross_terms(t_op, t_po)
    vv_own, oo_own = lax.psum((vv_own, oo_own), "aux")
    vv_cross, oo_cross = lax.psum((vv_cross, oo_cross), "aux")
    vv_total = vv_own + vv_cross
    oo_total = oo_own + oo_cross
    return (2.0 * vv_total, -2.0 * oo_total)


def solution(mesh):
    return jax.shard_map(
        shards,
        mesh=mesh,
        in_specs=(P("aux", "blk", None), P(), P()),
        out_specs=(P("blk", None), P("blk", None)),
        check_vma=False,
    )
```

profile of v0, /device:TPU:128, one launch (start us, length us, event | category | flops | bytes accessed | tf_op | source)
XLA Modules:
  0.0 903.5 jit_solution(79980119926642192)
XLA Ops:
  7.2 14.8 %copy.52 = bf16[200,2,4096]{0,1,2:T(2,128)(2,1)} copy(bf16[200,2,4096]{2,1,0:T(2,128)(2,1)} %param.3) | data formatting | bytes 6553600 | tf_op args[0]
  22.0 19.8 %all-to-all-start = ((bf16[200,2,4096]{0,1,2:T(2,128)(2,1)}), bf16[200,2,4096]{0,1,2:T(2,128)(2,1)}, u32[]{:S(2)}, u32[]{:S(2)}) async-start(bf16[200,2,4096]{0,1,2:T(2,128)(2,1)} %copy.52), calls=%async_computation | async-start | bytes 8388608 | tf_op jit(solution)/shard_map/all_to_all | solution.py:60
  41.8 0.7 copy.76
  42.6 296.2 %all-gather.3.cloned.1.call-done = bf16[64,200,192]{1,2,0:T(8,128)(2,1)} async-done(((bf16[1,200,192]{1,2,0:T(8,128)(2,1)}), bf16[64,200,192]{1,2,0:T(8,128)(2,1)}) %all-gather.3.cloned.1.call-update) | async-done | bytes 4915216 | tf_op jit(solution)/shard_map/all_gather | solution.py:64
  338.8 9.0 copy.51
  347.7 12.6 %reshape.138 = bf16[12800,192]{0,1:T(8,128)(2,1)} reshape(bf16[64,200,192]{1,0,2:T(8,128)(2,1)} %copy.51) | data formatting | bytes 9830400
  360.3 1.9 collective-permute-start.1
  362.2 2.7 copy.53
  365.0 4.5 copy.54
  369.5 8.5 reshape.135
  377.9 2.1 collective-permute-start
  380.1 0.1 dynamic_slice.10
  380.1 0.1 fusion.12
  380.2 0.1 broadcast_add_fusion
  380.3 0.1 broadcast_subtract_fusion.3
  380.4 39.5 %collective-permute-done.1 = bf16[12800,192]{0,1:T(8,128)(2,1)} collective-permute-done((bf16[12800,192]{0,1:T(8,128)(2,1)}, bf16[12800,192]{0,1:T(8,128)(2,1)}, u32[]{:S(2)}, u32[]{:S(2)}) %collective-permute-start.1) | collective-permute-done | bytes 4915232 | tf_op jit(solution)/shard_map/ppermute | solution.py:11
  419.9 5.5 fusion.14
  425.5 0.1 copy-done
  425.5 2.0 broadcast_subtract_fusion
  427.5 27.5 %collective-permute-done = bf16[12800,128]{0,1:T(8,128)(2,1)} collective-permute-done((bf16[12800,128]{0,1:T(8,128)(2,1)}, bf16[12800,128]{0,1:T(8,128)(2,1)}, u32[]{:S(2)}, u32[]{:S(2)}) %collective-permute-start) | collective-permute-done | bytes 3276832 | tf_op jit(solution)/shard_map/ppermute | solution.py:11
  455.0 3.6 fusion.13
  458.6 0.1 reshape.136
  458.7 0.1 fusion.3
  458.9 0.1 bitcast_subtract_fusion
  458.9 0.2 convolution_bitcast_fusion
  459.1 0.3 convolution_bitcast_fusion.3
  459.4 0.2 fusion.1
  459.6 0.2 fusion.2
  459.9 0.2 fusion
  460.1 435.4 %all-reduce = (f32[96,96]{1,0:T(8,128)S(1)}, f32[2,2]{1,0:T(2,128)S(1)}) all-reduce(f32[96,96]{1,0:T(8,128)S(1)} %fusion, f32[2,2]{1,0:T(2,128)S(1)} %fusion.2), channel_id=1, replica_groups=mesh['blk'=8,'aux'=64] {'aux'}, use_global_device_ids=true, to_apply=%region_0.1 | all-reduce | flops 9220 | bytes 73760 | tf_op jit(solution)/shard_map/psum | solution.py:74
  895.5 0.6 broadcast_multiply_fusion
  896.1 0.6 broadcast_multiply_fusion.1
  (19 shorter events, 0.1 us)
Async XLA Ops:
  22.0 19.9 %slice-start.2 = ((bf16[200,2,4096]{2,1,0:T(2,128)(2,1)}), bf16[200,2,96]{2,1,0:T(2,128)(2,1)S(1)}, s32[]{:S(2)}) async-start(bf16[200,2,4096]{2,1,0:T(2,128)(2,1)} %param.3), calls=%async_computation.4 | async-start | bytes 204800 | tf_op jit(solution)/shard_map/slice | solution.py:59
  22.0 340.3 %all-to-all-start = ((bf16[200,2,4096]{0,1,2:T(2,128)(2,1)}), bf16[200,2,4096]{0,1,2:T(2,128)(2,1)}, u32[]{:S(2)}, u32[]{:S(2)}) async-start(bf16[200,2,4096]{0,1,2:T(2,128)(2,1)} %copy.52), calls=%async_computation | async-start | bytes 8388608 | tf_op jit(solution)/shard_map/all_to_all | solution.py:60
  41.8 297.0 %all-gather.3.cloned.1.call-start = ((), (), s32[]{:S(2)}) async-start(), calls=%async_computation.1 | async-start | bytes 6389760 | tf_op jit(solution)/shard_map/all_gather | solution.py:64
  360.3 59.7 %collective-permute-start.1 = (bf16[12800,192]{0,1:T(8,128)(2,1)}, bf16[12800,192]{0,1:T(8,128)(2,1)}, u32[]{:S(2)}, u32[]{:S(2)}) collective-permute-start(bf16[12800,192]{0,1:T(8,128)(2,1)} %reshape.138), channel_id=1, source_target_pairs={{0,64},{64,128},{128,192},{192,256},{256,320},{320,384},{384,448},... | collective-permute-start | bytes 14745608 | tf_op jit(solution)/shard_map/ppermute | solution.py:11
  369.5 10.6 %copy-start.2 = (f32[4096]{0:T(1024)S(1)}, f32[4096]{0:T(1024)}, u32[]{:S(2)}) copy-start(f32[4096]{0:T(1024)} %param.5) | copy-start | bytes 49156
  369.5 10.7 %copy-start.1 = (f32[16]{0:T(128)S(1)}, f32[16]{0:T(128)}, u32[]{:S(2)}) copy-start(f32[16]{0:T(128)} %param.4) | copy-start | bytes 196
  369.5 10.8 %slice-start.3 = ((f32[4096]{0:T(1024)}), f32[96]{0:T(128)S(1)}, s32[]{:S(2)}) async-start(f32[4096]{0:T(1024)} %param.5), calls=%async_computation.5 | async-start | bytes 1024 | tf_op jit(solution)/shard_map/slice | solution.py:55
  369.5 56.0 %slice-start = ((s8[4915200]{0:T(1024)(128)(4,1)}), s8[720896]{0:T(1024)(128)(4,1)S(1)}, s32[]{:S(2)}) async-start(s8[4915200]{0:T(1024)(128)(4,1)} %bitcast.77), calls=%async_computation.2 | async-start | bytes 1441792
  377.9 77.1 %collective-permute-start = (bf16[12800,128]{0,1:T(8,128)(2,1)}, bf16[12800,128]{0,1:T(8,128)(2,1)}, u32[]{:S(2)}, u32[]{:S(2)}) collective-permute-start(bf16[12800,128]{0,1:T(8,128)(2,1)} %reshape.135), channel_id=1, source_target_pairs={{0,64},{64,128},{128,192},{192,256},{256,320},{320,384},{384,448},... | collective-permute-start | bytes 9830408 | tf_op jit(solution)/shard_map/ppermute | solution.py:11
  419.9 5.5 slice-start.1
  419.9 5.6 copy-start
Sparse Core Ops, SparseCore 0:
  46.7 292.0 all-gather.2
where the time goes:
time: 905 us; the launch traced here: 903 us
  blocking collectives  435 us (48%)
  waiting for transfers between devices  363 us (40%)
  local copies, waits for them, and re-layouts  53.1 us (6%)
  starting transfers between devices  23.9 us (3%)
  between operations  14.2 us (2%)
  matrix products  12.1 us (1%)
    psum x1, blocking collectives, shards(): vv_own, oo_own = lax.psum((vv_own, oo_own), 'aux')  435 us
    all_gather x1, waiting for transfers between devices, shards(): slab_all = lax.all_gather(slab_local, 'aux', axis=0, tiled=True)  296 us
    ppermute x2, waiting for transfers between devices, shifted(): lax.ppermute(x, axis, [(i, (i + by) % devices) for i in range(devices)])  67.1 us
    unnamed x13, local copies, waits for them, and re-layouts  28.2 us
    all_to_all x1, starting transfers between devices, shards(): lax.all_to_all(three_index, 'aux', split_axis=2, concat_axis=0, tiled=True)  19.8 us
  transfers between devices with their start and end apart: 4, of which 3 were waited for; matrix products, arithmetic and copies ran while one was open for 5% of the time, Pallas kernels for 0%

commit v1 on v0

v1 whole, which is shorter than its diff:
```python
import functools

import jax
import jax.numpy as jnp
from jax import lax
from jax.experimental import pallas as pl
from jax.experimental.pallas import tpu as pltpu
from jax.sharding import PartitionSpec as P

MESH = pl.DeviceIdType.MESH
AW = 96
LANE = 128
CHUNKS = 4
TILES = 2
N = 4
WIDE = 1024
OPW = 4 * AW
RESTW = WIDE - OPW
LINK = jnp.bfloat16
F32 = jnp.float32


def spread(raw):
    rows = lax.broadcasted_iota(jnp.int32, raw.shape, 0)
    even = lax.rem(rows, 2) == 0
    zero = jnp.zeros_like(raw)
    up = jnp.concatenate([raw[1:], raw[:1]], axis=0)
    down = jnp.concatenate([raw[-1:], raw[:-1]], axis=0)
    f00 = jnp.where(even, raw, zero)
    f11 = jnp.where(even, zero, raw)
    f10 = jnp.where(even, up, zero)
    f01 = jnp.where(even, zero, down)
    return [f[:, :AW] for f in (f00, f01, f10, f11)]


def kernel(
    x_ref, occ_ref, vir_ref, vv_ref, oo_ref,
    xb, sl, sw, pb, yb, sb, zop, zrest, tb, va, vb, vc, vd,
    loc_sem, xs, xr, ss, sr, ys, yr, os_, or_, rs, rr, vs, vr,
):
    g = lax.axis_index("blk")
    aux = lax.axis_index("aux")
    blocks = 8
    zh = aux // 16
    x = lax.rem(aux // 4, 4)
    y = lax.rem(aux, 4)
    nxt, prv = lax.rem(g + 1, blocks), lax.rem(g + blocks - 1, blocks)
    depth = x_ref.shape[0]
    rows = 2 * depth

    def at(z_, x_, y_, g_=None):
        return {"blk": g if g_ is None else g_, "aux": z_ * 16 + x_ * 4 + y_}

    def go(v, d):
        return lax.rem(v + d, N)

    peers = [at(zh, go(x, d), y) for d in (1, 2, 3)]
    peers += [at(zh, x, go(y, d)) for d in (1, 2, 3)]
    peers += [at(go(zh, d), x, y) for d in (1, 2, 3)]
    peers += [at(go(zh, d), x, y, h) for h in (nxt, prv) for d in (0, 1, 2, 3)]
    barrier = pltpu.get_barrier_semaphore()
    for peer in peers:
        pl.semaphore_signal(barrier, inc=1, device_id=peer, device_id_type=MESH)
    pl.semaphore_wait(barrier, len(peers))

    def remote(src, dst, send, recv, peer):
        return pltpu.make_async_remote_copy(
            src_ref=src, dst_ref=dst, send_sem=send, recv_sem=recv, device_id=peer, device_id_type=MESH
        )

    sends = []
    own_slab = pltpu.make_async_copy(x_ref.at[:, 0], sl.at[0, 0], loc_sem.at[0])
    own_slab.start()
    slab_x = []
    for d in (1, 2, 3):
        c = remote(x_ref.at[:, 0], sl.at[0, d], ss.at[0, d], sr.at[0, d], at(zh, go(x, d), y))
        c.start()
        slab_x.append(c)

    def forward(src, d):
        out = []
        for group, h in ((2, nxt), (1, prv)):
            c = remote(src, sl.at[group, d], ss.at[group, d], sr.at[group, d], at(zh, x, y, h))
            c.start()
            out.append(c)
        return out

    slab_f = forward(x_ref.at[:, 0], 0)

    tiles = {}
    locals_ = {}
    for c in range(CHUNKS):
        for l in range(TILES):
            for d in (1, 2, 3):
                lt = (c * N + go(x, d)) * TILES + l
                cp = remote(
                    x_ref.at[:, lt], xb.at[c, l, d], xs.at[c, l, d], xr.at[c, l, d], at(zh, go(x, d), y)
                )
                cp.start()
                tiles[c, l, d] = cp
            lt = (c * N + x) * TILES + l
            cp = pltpu.make_async_copy(x_ref.at[:, lt], xb.at[c, l, 0], loc_sem.at[1 + c * TILES + l])
            cp.start()
            locals_[c, l] = cp

    own_slab.wait()
    for d in (1, 2, 3):
        slab_x[d - 1].wait_recv()
        slab_f += forward(sl.at[0, d], d)

    for cp in slab_f:
        cp.wait_recv()
    for d in range(N):
        own = spread(sl.at[0, d].reshape(rows, LANE)[...].astype(F32))
        nex = spread(sl.at[1, d].reshape(rows, LANE)[...].astype(F32))
        pre = spread(sl.at[2, d].reshape(rows, LANE)[...].astype(F32))
        pad = jnp.zeros((rows, WIDE - 10 * AW), F32)
        sw[pl.ds(d * rows, rows), :] = jnp.concatenate(nex + pre + [own[1], own[2], pad], axis=1).astype(jnp.bfloat16)

    per = TILES * LANE // N
    fin = per // N
    y_copies, z_copies, z_local = {}, {}, {}

    def multiply(c):
        for l in range(TILES):
            for d in (1, 2, 3):
                tiles[c, l, d].wait_recv()
            locals_[c, l].wait()
            block = xb.at[c, l].reshape(N * rows, LANE)[...]
            prod = lax.dot_general(block, sw[...], (((0,), (0,)), ((), ())), preferred_element_type=F32)
            pb[c, pl.ds(l * LANE, LANE), :] = prod.astype(LINK)
        for d in (1, 2, 3):
            yy = go(y, d)
            cp = remote(
                pb.at[c, pl.ds(pl.multiple_of(yy * per, per), per)], yb.at[c, d - 1],
                ys.at[c, d - 1], yr.at[c, d - 1], at(zh, x, yy),
            )
            cp.start()
            y_copies[c, d] = cp

    def reduce_y(c):
        for d in (1, 2, 3):
            y_copies[c, d].wait_recv()
        total = pb[c, pl.ds(pl.multiple_of(y * per, per), per), :].astype(F32)
        for d in range(3):
            total = total + yb[c, d].astype(F32)
        sb[c] = total.astype(LINK)
        for d in range(N):
            zz = go(zh, d)
            part = pl.ds(pl.multiple_of(zz * fin, fin), fin)
            cp = remote(
                sb.at[c, part, pl.ds(0, OPW)], zop.at[c, d], os_.at[c, d], or_.at[c, d], at(zz, x, y, nxt)
            )
            cp.start()
            z_copies[c, d, 0] = cp
            if d == 0:
                cp = pltpu.make_async_copy(
                    sb.at[c, part, pl.ds(OPW, RESTW)], zrest.at[c, d], rr.at[c, d]
                )
                cp.start()
                z_local[c] = cp
            else:
                cp = remote(
                    sb.at[c, part, pl.ds(OPW, RESTW)], zrest.at[c, d], rs.at[c, d], rr.at[c, d], at(zz, x, y)
                )
                cp.start()
                z_copies[c, d, 1] = cp

    def reduce_z(c):
        z_local[c].wait()
        for d in range(N):
            z_copies[c, d, 0].wait_recv()
            if d:
                z_copies[c, d, 1].wait_recv()
        first = zop[c, 0].astype(F32)
        second = zrest[c, 0].astype(F32)
        for d in (1, 2, 3):
            first = first + zop[c, d].astype(F32)
            second = second + zrest[c, d].astype(F32)
        tb[pl.ds(c * fin, fin), pl.ds(0, OPW)] = first
        tb[pl.ds(c * fin, fin), pl.ds(OPW, RESTW)] = second

    for step in range(CHUNKS + 2):
        if step < CHUNKS:
            multiply(step)
        if 0 <= step - 1 < CHUNKS:
            reduce_y(step - 1)
        if 0 <= step - 2 < CHUNKS:
            reduce_z(step - 2)

    lane = lax.broadcasted_iota(jnp.int32, (fin, LANE), 1)
    row = lax.broadcasted_iota(jnp.int32, (fin, LANE), 0)
    offset = lax.rem(y, 2) * per + zh * fin
    columns = []
    for c in range(CHUNKS):
        lt = (c * N + x) * TILES + y // 2
        line = jnp.broadcast_to(vir_ref[pl.ds(lt, 1), :], (fin, LANE))
        columns.append(jnp.sum(jnp.where(lane == row + offset, line, 0.0), axis=1, keepdims=True))
    eb = jnp.concatenate(columns, axis=0)
    ea = vir_ref[0:1, 0:AW]
    eo = [occ_ref[2 * g], occ_ref[2 * g + 1]]
    ep = [occ_ref[2 * prv], occ_ref[2 * prv + 1]]

    def amplitude(k, ei, ej):
        return tb[:, k * AW:(k + 1) * AW] / (((ei + ej) - ea) - eb)

    op = [[amplitude(2 * i + j, eo[i], ep[j]) for j in range(2)] for i in range(2)]
    po = [[amplitude(4 + 2 * i + j, ep[i], eo[j]) for j in range(2)] for i in range(2)]
    ow = [amplitude(8, eo[0], eo[1]), amplitude(9, eo[1], eo[0])]
    mop = [[2.0 * op[i][j] - po[j][i] for j in range(2)] for i in range(2)]
    mpo = [[2.0 * po[i][j] - op[j][i] for j in range(2)] for i in range(2)]
    mow = [2.0 * ow[0] - ow[1], 2.0 * ow[1] - ow[0]]
    left = jnp.concatenate(op[0] + op[1] + po[0] + po[1] + ow, axis=0)
    right = jnp.concatenate(mop[0] + mop[1] + mpo[0] + mpo[1] + mow, axis=0)
    vv = lax.dot_general(
        left, right, (((0,), (0,)), ((), ())), preferred_element_type=F32, precision=lax.Precision.HIGHEST
    )

    def inner(a, b):
        return jnp.sum(jnp.sum(a * b, axis=1, keepdims=True), axis=0, keepdims=True)

    oo = []
    for i in range(2):
        for j in range(2):
            s = inner(op[i][0], mop[j][0]) + inner(op[i][1], mop[j][1])
            if i == j:
                s = s + inner(ow[i], mow[i])
            oo.append(s)
    corner = jnp.zeros((AW, LANE - AW), F32)
    cl = lax.broadcasted_iota(jnp.int32, corner.shape, 1)
    for k in range(4):
        corner = jnp.where(cl == k, jnp.broadcast_to(oo[k], corner.shape), corner)
    va[...] = jnp.concatenate([2.0 * vv, -2.0 * corner], axis=1)

    piece = AW // N
    fin_copies = []
    group = []
    for d in (1, 2, 3):
        yy = go(y, d)
        cp = remote(
            va.at[pl.ds(pl.multiple_of(yy * piece, 8), piece)], vb.at[d - 1], vs.at[0, d], vr.at[0, d], at(zh, x, yy)
        )
        cp.start()
        group.append(cp)
    for cp in group:
        cp.wait_recv()
    fin_copies += group
    total = va[pl.ds(pl.multiple_of(y * piece, 8), piece), :]
    for d in range(3):
        total = total + vb[d]

    def everyone(total, buf, stage, me, where):
        buf[me] = total
        group = []
        for d in (1, 2, 3):
            cp = remote(buf.at[me], buf.at[me], vs.at[stage, d], vr.at[stage, d], where(d))
            cp.start()
            group.append(cp)
        for cp in group:
            cp.wait_recv()
        return group

    fin_copies += everyone(total, vc.at[0], 1, x, lambda d: at(zh, go(x, d), y))
    total = (vc[0, 0] + vc[0, 1]) + (vc[0, 2] + vc[0, 3])
    fin_copies += everyone(total, vc.at[1], 2, zh, lambda d: at(go(zh, d), x, y))
    total = (vc[1, 0] + vc[1, 1]) + (vc[1, 2] + vc[1, 3])
    fin_copies += everyone(total, vd, 3, y, lambda d: at(zh, x, go(y, d)))
    for k in range(N):
        vv_ref[pl.ds(k * piece, piece), :] = vd[k][:, :AW]
    tail = vd[0][0:1, AW:]
    oo_ref[...] = jnp.concatenate([tail[:, 0:2], tail[:, 2:4]], axis=0)

    for group in (slab_x, slab_f, tiles.values(), y_copies.values(), z_copies.values(), fin_copies):
        for cp in group:
            cp.wait_send()


def shards(three_index, occ_energy, vir_energy):
    depth, occ, vir = three_index.shape
    tiles = vir // LANE
    view = three_index.reshape(depth, occ, tiles, LANE).transpose(0, 2, 1, 3)
    bf16 = jnp.bfloat16
    per = TILES * LANE // N
    fin = per // N
    piece = AW // N
    dma = pltpu.SemaphoreType.DMA
    return pl.pallas_call(
        kernel,
        out_shape=(jax.ShapeDtypeStruct((AW, AW), F32), jax.ShapeDtypeStruct((2, 2), F32)),
        in_specs=[
            pl.BlockSpec(memory_space=pl.ANY),
            pl.BlockSpec(memory_space=pltpu.SMEM),
            pl.BlockSpec(memory_space=pltpu.VMEM),
        ],
        out_specs=(pl.BlockSpec(memory_space=pltpu.VMEM), pl.BlockSpec(memory_space=pltpu.VMEM)),
        scratch_shapes=[
            pltpu.VMEM((CHUNKS, TILES, N, depth, occ, LANE), bf16),
            pltpu.VMEM((3, N, depth, occ, LANE), bf16),
            pltpu.VMEM((N * depth * occ, WIDE), bf16),
            pltpu.VMEM((CHUNKS, TILES * LANE, WIDE), LINK),
            pltpu.VMEM((CHUNKS, 3, per, WIDE), LINK),
            pltpu.VMEM((CHUNKS, per, WIDE), LINK),
            pltpu.VMEM((CHUNKS, N, fin, OPW), LINK),
            pltpu.VMEM((CHUNKS, N, fin, RESTW), LINK),
            pltpu.VMEM((CHUNKS * fin, WIDE), F32),
            pltpu.VMEM((AW, LANE), F32),
            pltpu.VMEM((3, piece, LANE), F32),
            pltpu.VMEM((2, N, piece, LANE), F32),
            pltpu.VMEM((N, piece, LANE), F32),
            dma((1 + CHUNKS * TILES,)),
            dma((CHUNKS, TILES, N)), dma((CHUNKS, TILES, N)),
            dma((3, N)), dma((3, N)),
            dma((CHUNKS, 3)), dma((CHUNKS, 3)),
            dma((CHUNKS, N)), dma((CHUNKS, N)),
            dma((CHUNKS, N)), dma((CHUNKS, N)),
            dma((4, N)), dma((4, N)),
        ],
        compiler_params=pltpu.CompilerParams(
            collective_id=0, has_side_effects=True, vmem_limit_bytes=56 * 1024 * 1024
        ),
        cost_estimate=pl.CostEstimate(flops=4_000_000_000, bytes_accessed=8_000_000, transcendentals=0),
    )(view, occ_energy, vir_energy.reshape(vir // LANE, LANE))


def solution(mesh):
    return jax.shard_map(
        shards,
        mesh=mesh,
        in_specs=(P("aux", "blk", None), P(), P()),
        out_specs=(P("blk", None), P("blk", None)),
        check_vma=False,
    )
```

time: 905 us -> 103 us (0.11)
  the two profiles are of different devices: /device:TPU:128 before, /device:TPU:2 now
where the time goes in v1:
time: 103 us
  Pallas kernels  99.6 us (97%)
  local copies, waits for them, and re-layouts  2.62 us (3%)
    pallas_call x1, Pallas kernels, shards(): pl.pallas_call(kernel, out_shape=(jax.ShapeDtypeStruct((AW, AW), F32), ja...  99.6 us
    unnamed x2, local copies, waits for them, and re-layouts  2.62 us

profile of v1, /device:TPU:2, one launch (start us, length us, event | category | flops | bytes accessed | tf_op | source)
XLA Modules:
  0.0 102.9 jit_solution(618235655406539884)
XLA Ops:
  0.6 99.6 %shard_map.50 = (f32[96,96]{1,0:T(8,128)}, f32[2,2]{1,0:T(2,128)}) custom-call(bf16[200,32,2,128]{3,2,1,0:T(2,128)(2,1)} %bitcast.4, f32[16]{0:T(128)} %occ_ref.1, f32[32,128]{1,0:T(8,128)} %bitcast.5), custom_call_target="tpu_custom_call" | custom-call | flops 4000000000 | bytes 8000000 | tf_op jit(solution)/shard_map/pallas_call | solution.py:287
  100.3 1.4 %copy.7 = f32[96,96]{1,0:T(8,128)} copy(f32[96,96]{1,0:T(8,128)} %get-tuple-element.4) | data formatting | bytes 73728
  101.7 1.2 %copy.8 = f32[2,2]{1,0:T(2,128)} copy(f32[2,2]{1,0:T(2,128)} %get-tuple-element.5) | data formatting | bytes 32

commit v2 on v1

v2 whole, which is shorter than its diff:
```python
import functools

import jax
import jax.numpy as jnp
from jax import lax
from jax.experimental import pallas as pl
from jax.experimental.pallas import tpu as pltpu
from jax.sharding import PartitionSpec as P

MESH = pl.DeviceIdType.MESH
AW = 96
LANE = 128
CHUNKS = 8
N = 4
WIDE = 1024
OPW = 4 * AW
RESTW = WIDE - OPW
LINK = jnp.bfloat16
F32 = jnp.float32


def spread(raw):
    rows = lax.broadcasted_iota(jnp.int32, raw.shape, 0)
    even = lax.rem(rows, 2) == 0
    zero = jnp.zeros_like(raw)
    up = jnp.concatenate([raw[1:], raw[:1]], axis=0)
    down = jnp.concatenate([raw[-1:], raw[:-1]], axis=0)
    f00 = jnp.where(even, raw, zero)
    f11 = jnp.where(even, zero, raw)
    f10 = jnp.where(even, up, zero)
    f01 = jnp.where(even, zero, down)
    return [f[:, :AW] for f in (f00, f01, f10, f11)]


def kernel(
    x_ref, occ_ref, vir_ref, out_ref,
    xb, sl, sw, pb, yb, sb, zop, zrest, tb, va, vb, vc, vd,
    loc_sem, xs, xr, ss, sr, ys, yr, os_, or_, rs, rr, vs, vr,
):
    g = lax.axis_index("blk")
    aux = lax.axis_index("aux")
    blocks = 8
    zh = aux // 16
    x = lax.rem(aux // 4, 4)
    y = lax.rem(aux, 4)
    nxt, prv = lax.rem(g + 1, blocks), lax.rem(g + blocks - 1, blocks)
    depth = x_ref.shape[0]
    rows = 2 * depth

    def at(z_, x_, y_, g_=None):
        return {"blk": g if g_ is None else g_, "aux": z_ * 16 + x_ * 4 + y_}

    def go(v, d):
        return lax.rem(v + d, N)

    peers = [at(go(zh, d), x, y, h) for d in (2, 1, 3) for h in (nxt, prv, g)]
    peers += [at(zh, go(x, d), y) for d in (2, 1, 3)]
    peers += [at(zh, x, go(y, d)) for d in (2, 1, 3)]
    peers += [at(zh, x, y, h) for h in (nxt, prv)]
    barrier = pltpu.get_barrier_semaphore()
    for peer in peers:
        pl.semaphore_signal(barrier, inc=1, device_id=peer, device_id_type=MESH)
    pl.semaphore_wait(barrier, len(peers))

    def remote(src, dst, send, recv, peer):
        return pltpu.make_async_remote_copy(
            src_ref=src, dst_ref=dst, send_sem=send, recv_sem=recv, device_id=peer, device_id_type=MESH
        )

    place = (x, y)

    def along(axis, d):
        return at(zh, go(x, d), y) if axis == 0 else at(zh, x, go(y, d))

    own_slab = pltpu.make_async_copy(x_ref.at[:, 0], sl.at[0, 0], loc_sem.at[0])
    own_slab.start()
    slab_p = {}
    for axis in (0, 1):
        for d in (2, 1, 3):
            k = 3 * axis + d
            cp = remote(x_ref.at[:, 0], sl.at[0, k], ss.at[0, k], sr.at[0, k], along(axis, d))
            cp.start()
            slab_p[k] = cp
    slab_f = {}

    def forward(src, k):
        for group, h, end in ((2, nxt, blocks - 1), (1, prv, 0)):
            cp = remote(src, sl.at[group, k], ss.at[group, k], sr.at[group, k], at(zh, x, y, h))
            if k == 0:
                cp.start()
            else:
                pl.when(g != end)(cp.start)
            slab_f[group, k] = cp

    def gather(group, end):
        slab_f[group, 0].wait_recv()

        @pl.when(g == end)
        def _():
            for k in (2, 5, 1, 4, 3, 6):
                remote(
                    sl.at[group, 0], sl.at[group, k], ss.at[3 - group, k], sr.at[group, k],
                    along((k - 1) // 3, (k - 1) % 3 + 1),
                ).start()

    forward(x_ref.at[:, 0], 0)

    tiles = {}
    locals_ = {}

    def exchange(*chunks):
        for c in chunks:
            axis = c % 2
            for d in (2, 1, 3):
                lt = c * N + go(place[axis], d)
                cp = remote(x_ref.at[:, lt], xb.at[c, d], xs.at[c, d], xr.at[c, d], along(axis, d))
                cp.start()
                tiles[c, d] = cp
            cp = pltpu.make_async_copy(x_ref.at[:, c * N + place[axis]], xb.at[c, 0], loc_sem.at[1 + c])
            cp.start()
            locals_[c] = cp

    exchange(0, 1)
    gather(2, 0)
    gather(1, blocks - 1)
    for k in (1, 4, 3, 6, 2, 5):
        slab_p[k].wait_recv()
        forward(sl.at[0, k], k)
    exchange(2, 3)
    own_slab.wait()

    for k in (0, 1, 4, 3, 6, 2, 5):
        if k:
            slab_f[1, k].wait_recv()
            slab_f[2, k].wait_recv()
        own, nex, pre = [spread(sl.at[r, k].reshape(rows, LANE)[...].astype(F32)) for r in range(3)]
        pad = jnp.zeros((rows, WIDE - 10 * AW), F32)
        wide = jnp.concatenate(nex + pre + [own[1], own[2], pad], axis=1).astype(jnp.bfloat16)
        if k < 4:
            sw[0, pl.ds(k * rows, rows), :] = wide
        if k > 3:
            sw[1, pl.ds((k - 3) * rows, rows), :] = wide
        if k == 0:
            sw[1, pl.ds(0, rows), :] = wide

    per = LANE // N
    fin = per // N
    y_copies, z_copies, z_local = {}, {}, {}

    def multiply(c):
        axis = c % 2
        for d in (1, 2, 3):
            tiles[c, d].wait_recv()
        locals_[c].wait()
        block = xb.at[c].reshape(N * rows, LANE)[...]
        prod = lax.dot_general(block, sw[axis], (((0,), (0,)), ((), ())), preferred_element_type=F32)
        for k in range(N):
            pb[c, k] = prod[k * per:(k + 1) * per].astype(LINK)
        for d in (2, 1, 3):
            cp = remote(
                pb.at[c, go(place[1 - axis], d)], yb.at[c, d - 1], ys.at[c, d - 1], yr.at[c, d - 1], along(1 - axis, d)
            )
            cp.start()
            y_copies[c, d] = cp

    def reduce_y(c):
        for d in (1, 2, 3):
            y_copies[c, d].wait_recv()
        total = pb[c, place[1 - c % 2]].astype(F32)
        for d in range(3):
            total = total + yb[c, d].astype(F32)
        for k in range(N):
            sb[c, k] = total[k * fin:(k + 1) * fin].astype(LINK)
        for d in (2, 1, 3, 0):
            zz = go(zh, d)
            cp = remote(sb.at[c, zz, :, pl.ds(0, OPW)], zop.at[c, d], os_.at[c, d], or_.at[c, d], at(zz, x, y, nxt))
            cp.start()
            z_copies[c, d, 0] = cp
            src = sb.at[c, zz, :, pl.ds(OPW, RESTW)]
            if d == 0:
                cp = pltpu.make_async_copy(src, zrest.at[c, d], rr.at[c, d])
                cp.start()
                z_local[c] = cp
            else:
                cp = remote(src, zrest.at[c, d], rs.at[c, d], rr.at[c, d], at(zz, x, y))
                cp.start()
                z_copies[c, d, 1] = cp

    def reduce_z(c):
        z_local[c].wait()
        for d in range(N):
            z_copies[c, d, 0].wait_recv()
            if d:
                z_copies[c, d, 1].wait_recv()
        first = zop[c, 0].astype(F32)
        second = zrest[c, 0].astype(F32)
        for d in (1, 2, 3):
            first = first + zop[c, d].astype(F32)
            second = second + zrest[c, d].astype(F32)
        tb[pl.ds(c * fin, fin), pl.ds(0, OPW)] = first
        tb[pl.ds(c * fin, fin), pl.ds(OPW, RESTW)] = second

    def run(step, *chunks):
        for c in chunks:
            step(c)

    run(multiply, 0, 1)
    exchange(4, 5)
    run(multiply, 2, 3)
    exchange(6, 7)
    run(reduce_y, 0, 1, 2, 3)
    run(multiply, 4, 5, 6, 7)
    run(reduce_y, 4, 5)
    run(reduce_z, 0, 1, 2, 3)
    run(reduce_y, 6, 7)
    run(reduce_z, 4, 5, 6, 7)

    lane = lax.broadcasted_iota(jnp.int32, (fin, LANE), 1)
    row = lax.broadcasted_iota(jnp.int32, (fin, LANE), 0)
    columns = []
    for c in range(CHUNKS):
        lt = c * N + place[c % 2]
        offset = place[1 - c % 2] * per + zh * fin
        line = jnp.broadcast_to(vir_ref[pl.ds(lt, 1), :], (fin, LANE))
        columns.append(jnp.sum(jnp.where(lane == row + offset, line, 0.0), axis=1, keepdims=True))
    eb = jnp.concatenate(columns, axis=0)
    ea = vir_ref[0:1, 0:AW]
    eo = [occ_ref[2 * g], occ_ref[2 * g + 1]]
    ep = [occ_ref[2 * prv], occ_ref[2 * prv + 1]]

    def amplitude(k, ei, ej):
        return tb[:, k * AW:(k + 1) * AW] / (((ei + ej) - ea) - eb)

    op = [[amplitude(2 * i + j, eo[i], ep[j]) for j in range(2)] for i in range(2)]
    po = [[amplitude(4 + 2 * i + j, ep[i], eo[j]) for j in range(2)] for i in range(2)]
    ow = [amplitude(8, eo[0], eo[1]), amplitude(9, eo[1], eo[0])]
    mop = [[2.0 * op[i][j] - po[j][i] for j in range(2)] for i in range(2)]
    mpo = [[2.0 * po[i][j] - op[j][i] for j in range(2)] for i in range(2)]
    mow = [2.0 * ow[0] - ow[1], 2.0 * ow[1] - ow[0]]
    left = jnp.concatenate(op[0] + op[1] + po[0] + po[1] + ow, axis=0)
    right = jnp.concatenate(mop[0] + mop[1] + mpo[0] + mpo[1] + mow, axis=0)
    vv = lax.dot_general(
        left, right, (((0,), (0,)), ((), ())), preferred_element_type=F32, precision=lax.Precision.HIGHEST
    )

    def inner(a, b):
        return jnp.sum(jnp.sum(a * b, axis=1, keepdims=True), axis=0, keepdims=True)

    oo = []
    for i in range(2):
        for j in range(2):
            s = inner(op[i][0], mop[j][0]) + inner(op[i][1], mop[j][1])
            if i == j:
                s = s + inner(ow[i], mow[i])
            oo.append(s)
    corner = jnp.zeros((AW, LANE - AW), F32)
    cl = lax.broadcasted_iota(jnp.int32, corner.shape, 1)
    for k in range(4):
        corner = jnp.where(cl == k, jnp.broadcast_to(oo[k], corner.shape), corner)
    va[...] = jnp.concatenate([2.0 * vv, -2.0 * corner], axis=1)

    piece = AW // N
    fin_copies = []
    group = []
    for d in (1, 2, 3):
        yy = go(y, d)
        cp = remote(
            va.at[pl.ds(pl.multiple_of(yy * piece, 8), piece)], vb.at[d - 1], vs.at[0, d], vr.at[0, d], at(zh, x, yy)
        )
        cp.start()
        group.append(cp)
    for cp in group:
        cp.wait_recv()
    fin_copies += group
    total = va[pl.ds(pl.multiple_of(y * piece, 8), piece), :]
    for d in range(3):
        total = total + vb[d]

    def everyone(total, buf, stage, me, where):
        buf[me] = total
        group = []
        for d in (1, 2, 3):
            cp = remote(buf.at[me], buf.at[me], vs.at[stage, d], vr.at[stage, d], where(d))
            cp.start()
            group.append(cp)
        for cp in group:
            cp.wait_recv()
        return group

    fin_copies += everyone(total, vc.at[0], 1, x, lambda d: at(zh, go(x, d), y))
    total = (vc[0, 0] + vc[0, 1]) + (vc[0, 2] + vc[0, 3])
    fin_copies += everyone(total, vc.at[1], 2, zh, lambda d: at(go(zh, d), x, y))
    total = (vc[1, 0] + vc[1, 1]) + (vc[1, 2] + vc[1, 3])
    fin_copies += everyone(total, vd, 3, y, lambda d: at(zh, x, go(y, d)))
    for k in range(N):
        out_ref[pl.ds(k * piece, piece), :] = vd[k]

    for group in (slab_p.values(), slab_f.values(), tiles.values(), y_copies.values(), z_copies.values(), fin_copies):
        for cp in group:
            cp.wait_send()


def shards(three_index, occ_energy, vir_energy):
    depth, occ, vir = three_index.shape
    tiles = vir // LANE
    view = three_index.reshape(depth, occ, tiles, LANE).transpose(0, 2, 1, 3)
    bf16 = jnp.bfloat16
    per = LANE // N
    fin = per // N
    piece = AW // N
    dma = pltpu.SemaphoreType.DMA
    out = pl.pallas_call(
        kernel,
        out_shape=jax.ShapeDtypeStruct((AW, LANE), F32),
        in_specs=[
            pl.BlockSpec(memory_space=pl.ANY),
            pl.BlockSpec(memory_space=pltpu.SMEM),
            pl.BlockSpec(memory_space=pltpu.VMEM),
        ],
        out_specs=pl.BlockSpec(memory_space=pltpu.VMEM),
        scratch_shapes=[
            pltpu.VMEM((CHUNKS, N, depth, occ, LANE), bf16),
            pltpu.VMEM((3, 7, depth, occ, LANE), bf16),
            pltpu.VMEM((2, N * depth * occ, WIDE), bf16),
            pltpu.VMEM((CHUNKS, N, per, WIDE), LINK),
            pltpu.VMEM((CHUNKS, 3, per, WIDE), LINK),
            pltpu.VMEM((CHUNKS, N, fin, WIDE), LINK),
            pltpu.VMEM((CHUNKS, N, fin, OPW), LINK),
            pltpu.VMEM((CHUNKS, N, fin, RESTW), LINK),
            pltpu.VMEM((CHUNKS * fin, WIDE), F32),
            pltpu.VMEM((AW, LANE), F32),
            pltpu.VMEM((3, piece, LANE), F32),
            pltpu.VMEM((2, N, piece, LANE), F32),
            pltpu.VMEM((N, piece, LANE), F32),
            dma((1 + CHUNKS,)),
            dma((CHUNKS, N)), dma((CHUNKS, N)),
            dma((3, 7)), dma((3, 7)),
            dma((CHUNKS, 3)), dma((CHUNKS, 3)),
            dma((CHUNKS, N)), dma((CHUNKS, N)),
            dma((CHUNKS, N)), dma((CHUNKS, N)),
            dma((4, N)), dma((4, N)),
        ],
        compiler_params=pltpu.CompilerParams(
            collective_id=0, has_side_effects=True, vmem_limit_bytes=56 * 1024 * 1024
        ),
        cost_estimate=pl.CostEstimate(flops=4_000_000_000, bytes_accessed=8_000_000, transcendentals=0),
    )(view, occ_energy, vir_energy.reshape(vir // LANE, LANE))
    return out[:, :AW], out[0, AW:AW + 4].reshape(2, 2)


def solution(mesh):
    return jax.shard_map(
        shards,
        mesh=mesh,
        in_specs=(P("aux", "blk", None), P(), P()),
        out_specs=(P("blk", None), P("blk", None)),
        check_vma=False,
    )
```

time: 103 us -> 97.7 us (0.949)
  the two profiles are of different devices: /device:TPU:2 before, /device:TPU:32 now
where the time goes in v2:
time: 97.7 us; the launch traced here: 97.4 us
  Pallas kernels  93.9 us (96%)
  local copies, waits for them, and re-layouts  2.83 us (3%)
    pallas_call x1, Pallas kernels, shards(): pl.pallas_call(kernel, out_shape=jax.ShapeDtypeStruct((AW, LANE), F32), i...  93.9 us

profile of v2, /device:TPU:32, one launch (start us, length us, event | category | flops | bytes accessed | tf_op | source)
XLA Modules:
  0.0 97.4 jit_solution(18209400235204693912)
XLA Ops:
  0.6 93.9 %shard_map.50 = f32[96,128]{1,0:T(8,128)} custom-call(bf16[200,32,2,128]{3,2,1,0:T(2,128)(2,1)} %bitcast.6, f32[16]{0:T(128)} %occ_ref.1, f32[32,128]{1,0:T(8,128)} %bitcast.7), custom_call_target="tpu_custom_call" | custom-call | flops 4000000000 | bytes 8000000 | tf_op jit(solution)/shard_map/pallas_call | solution.py:312
  94.6 0.8 slice_reduce_fusion
  95.3 0.6 reshape_squeeze.3
  96.0 1.4 %copy.6 = f32[96,96]{1,0:T(8,128)} copy(f32[96,96]{1,0:T(8,128)} %bitcast.5) | data formatting | bytes 73728

commit v3 on v2

--- a/solution.py
+++ b/solution.py
@@ -35,7 +35,7 @@
 def kernel(
     x_ref, occ_ref, vir_ref, out_ref,
     xb, sl, sw, pb, yb, sb, zop, zrest, tb, va, vb, vc, vd,
-    loc_sem, xs, xr, ss, sr, ys, yr, os_, or_, rs, rr, vs, vr,
+    loc_sem, xs, xr, ss, sr, ys, yr, os_, or_, rs, rr, vs, vr, ready,
 ):
     g = lax.axis_index("blk")
     aux = lax.axis_index("aux")
@@ -53,14 +53,32 @@
     def go(v, d):
         return lax.rem(v + d, N)
 
-    peers = [at(go(zh, d), x, y, h) for d in (2, 1, 3) for h in (nxt, prv, g)]
-    peers += [at(zh, go(x, d), y) for d in (2, 1, 3)]
-    peers += [at(zh, x, go(y, d)) for d in (2, 1, 3)]
-    peers += [at(zh, x, y, h) for h in (nxt, prv)]
+    def signal(sem, peer):
+        pl.semaphore_signal(sem, inc=1, device_id=peer, device_id_type=MESH)
+
+    def rank(v):
+        return v // 2 * 2 + lax.rem(v + v // 2, 2)
+
+    mine = rank(zh)
     barrier = pltpu.get_barrier_semaphore()
-    for peer in peers:
-        pl.semaphore_signal(barrier, inc=1, device_id=peer, device_id_type=MESH)
-    pl.semaphore_wait(barrier, len(peers))
+    near = [at(zh, go(x, d), y) for d in (2, 1, 3)]
+    near += [at(zh, x, go(y, d)) for d in (2, 1, 3)]
+    near += [at(zh, x, y, h) for h in (nxt, prv)]
+    for peer in near:
+        signal(barrier, peer)
+    for d in (2, 1, 3):
+        @pl.when(rank(go(zh, d)) > mine)
+        def _():
+            for h in (g, nxt, prv):
+                signal(barrier, at(go(zh, d), x, y, h))
+    pl.semaphore_wait(barrier, len(near) + 3 * mine)
+
+    def answer():
+        for d in (2, 1, 3):
+            @pl.when(rank(go(zh, d)) < mine)
+            def _():
+                for h in (g, prv):
+                    signal(ready, at(go(zh, d), x, y, h))
 
     def remote(src, dst, send, recv, peer):
         return pltpu.make_async_remote_copy(
@@ -126,26 +144,33 @@
     for k in (1, 4, 3, 6, 2, 5):
         slab_p[k].wait_recv()
         forward(sl.at[0, k], k)
-    exchange(2, 3)
+    exchange(2, 3, 4, 5)
+    answer()
     own_slab.wait()
 
+    def place_wide(k, start, forms):
+        wide = jnp.concatenate(forms, axis=1).astype(jnp.bfloat16)
+        for axis in (0, 1):
+            if k == 0 or (k - 1) // 3 == axis:
+                slot = 0 if k == 0 else k - 3 * axis
+                sw[axis, pl.ds(slot * rows, rows), pl.ds(start, wide.shape[1])] = wide
+
+    def forms(group, k):
+        return spread(sl.at[group, k].reshape(rows, LANE)[...].astype(F32))
+
+    pad = jnp.zeros((rows, WIDE - 10 * AW), F32)
+    for k in range(7):
+        own = forms(0, k)
+        place_wide(k, 2 * OPW, [own[1], own[2], pad])
     for k in (0, 1, 4, 3, 6, 2, 5):
-        if k:
-            slab_f[1, k].wait_recv()
-            slab_f[2, k].wait_recv()
-        own, nex, pre = [spread(sl.at[r, k].reshape(rows, LANE)[...].astype(F32)) for r in range(3)]
-        pad = jnp.zeros((rows, WIDE - 10 * AW), F32)
-        wide = jnp.concatenate(nex + pre + [own[1], own[2], pad], axis=1).astype(jnp.bfloat16)
-        if k < 4:
-            sw[0, pl.ds(k * rows, rows), :] = wide
-        if k > 3:
-            sw[1, pl.ds((k - 3) * rows, rows), :] = wide
-        if k == 0:
-            sw[1, pl.ds(0, rows), :] = wide
+        for group, start in ((1, 0), (2, OPW)):
+            if k:
+                slab_f[group, k].wait_recv()
+            place_wide(k, start, forms(group, k))
 
     per = LANE // N
     fin = per // N
-    y_copies, z_copies, z_local = {}, {}, {}
+    y_copies, z_copies = {}, {}
 
     def multiply(c):
         axis = c % 2
@@ -163,57 +188,61 @@
             cp.start()
             y_copies[c, d] = cp
 
-    def reduce_y(c):
-        for d in (1, 2, 3):
-            y_copies[c, d].wait_recv()
-        total = pb[c, place[1 - c % 2]].astype(F32)
-        for d in range(3):
-            total = total + yb[c, d].astype(F32)
-        for k in range(N):
-            sb[c, k] = total[k * fin:(k + 1) * fin].astype(LINK)
+    def reduce_y(pair):
+        for c in (2 * pair, 2 * pair + 1):
+            for d in (1, 2, 3):
+                y_copies[c, d].wait_recv()
+            total = pb[c, place[1 - c % 2]].astype(F32)
+            for d in range(3):
+                total = total + yb[c, d].astype(F32)
+            for k in range(N):
+                sb[pair, k, c % 2] = total[k * fin:(k + 1) * fin].astype(LINK)
         for d in (2, 1, 3, 0):
             zz = go(zh, d)
-            cp = remote(sb.at[c, zz, :, pl.ds(0, OPW)], zop.at[c, d], os_.at[c, d], or_.at[c, d], at(zz, x, y, nxt))
-            cp.start()
-            z_copies[c, d, 0] = cp
-            src = sb.at[c, zz, :, pl.ds(OPW, RESTW)]
-            if d == 0:
-                cp = pltpu.make_async_copy(src, zrest.at[c, d], rr.at[c, d])
+            src = sb.at[pair, zz, :, :, pl.ds(0, OPW)]
+            cp = remote(src, zop.at[pair, d], os_.at[pair, d], or_.at[pair, d], at(zz, x, y, nxt))
+            cp.start()
+            z_copies[pair, d, 0] = cp
+            if d:
+                src = sb.at[pair, zz, :, :, pl.ds(OPW, RESTW)]
+                cp = remote(src, zrest.at[pair, d - 1], rs.at[pair, d], rr.at[pair, d], at(zz, x, y))
                 cp.start()
-                z_local[c] = cp
-            else:
-                cp = remote(src, zrest.at[c, d], rs.at[c, d], rr.at[c, d], at(zz, x, y))
-                cp.start()
-                z_copies[c, d, 1] = cp
-
-    def reduce_z(c):
-        z_local[c].wait()
-        for d in range(N):
-            z_copies[c, d, 0].wait_recv()
-            if d:
-                z_copies[c, d, 1].wait_recv()
-        first = zop[c, 0].astype(F32)
-        second = zrest[c, 0].astype(F32)
-        for d in (1, 2, 3):
-            first = first + zop[c, d].astype(F32)
-            second = second + zrest[c, d].astype(F32)
-        tb[pl.ds(c * fin, fin), pl.ds(0, OPW)] = first
-        tb[pl.ds(c * fin, fin), pl.ds(OPW, RESTW)] = second
-
-    def run(step, *chunks):
+                z_copies[pair, d, 1] = cp
+
+    def reduce_z(pair):
+        for cp in [z_copies[pair, d, j] for d in (0, 1, 3, 2) for j in (0, 1) if d or not j]:
+            cp.wait_recv()
+        for j in (0, 1):
+            first = zop[pair, 0, j].astype(F32)
+            second = sb[pair, zh, j, :, pl.ds(OPW, RESTW)].astype(F32)
+            for d in (1, 2, 3):
+                first = first + zop[pair, d, j].astype(F32)
+                second = second + zrest[pair, d - 1, j].astype(F32)
+            part = pl.ds((2 * pair + j) * fin, fin)
+            tb[part, pl.ds(0, OPW)] = first
+            tb[part, pl.ds(OPW, RESTW)] = second
+
+    def multiply_all(*chunks):
         for c in chunks:
-            step(c)
-
-    run(multiply, 0, 1)
-    exchange(4, 5)
-    run(multiply, 2, 3)
+            multiply(c)
+
+    multiply_all(0, 1, 2, 3)
+    multiply_all(4, 5)
     exchange(6, 7)
-    run(reduce_y, 0, 1, 2, 3)
-    run(multiply, 4, 5, 6, 7)
-    run(reduce_y, 4, 5)
-    run(reduce_z, 0, 1, 2, 3)
-    run(reduce_y, 6, 7)
-    run(reduce_z, 4, 5, 6, 7)
+
+    @pl.when(mine < N - 1)
+    def _():
+        pl.semaphore_wait(ready, 2 * (N - 1 - mine))
+
+    reduce_y(0)
+    reduce_y(1)
+    multiply_all(6, 7)
+    reduce_y(2)
+    reduce_z(0)
+    reduce_z(1)
+    reduce_y(3)
+    reduce_z(2)
+    reduce_z(3)
 
     lane = lax.broadcasted_iota(jnp.int32, (fin, LANE), 1)
     row = lax.broadcasted_iota(jnp.int32, (fin, LANE), 0)
@@ -255,8 +284,10 @@
             oo.append(s)
     corner = jnp.zeros((AW, LANE - AW), F32)
     cl = lax.broadcasted_iota(jnp.int32, corner.shape, 1)
+    cr = lax.broadcasted_iota(jnp.int32, corner.shape, 0)
     for k in range(4):
-        corner = jnp.where(cl == k, jnp.broadcast_to(oo[k], corner.shape), corner)
+        here = jnp.logical_and(cr == k // 2, cl == k % 2)
+        corner = jnp.where(here, jnp.broadcast_to(oo[k], corner.shape), corner)
     va[...] = jnp.concatenate([2.0 * vv, -2.0 * corner], axis=1)
 
     piece = AW // N
@@ -276,28 +307,32 @@
     for d in range(3):
         total = total + vb[d]
 
-    def everyone(total, buf, stage, me, where):
+    def everyone(total, buf, stage, me, where, meanwhile=()):
         buf[me] = total
         group = []
-        for d in (1, 2, 3):
+        for d in (2, 1, 3):
             cp = remote(buf.at[me], buf.at[me], vs.at[stage, d], vr.at[stage, d], where(d))
             cp.start()
             group.append(cp)
+        for copies in meanwhile:
+            for cp in copies:
+                cp.wait_send()
         for cp in group:
             cp.wait_recv()
         return group
 
-    fin_copies += everyone(total, vc.at[0], 1, x, lambda d: at(zh, go(x, d), y))
+    fin_copies += everyone(total, vc.at[0], 1, x, lambda d: at(zh, go(x, d), y), (slab_p.values(), slab_f.values()))
     total = (vc[0, 0] + vc[0, 1]) + (vc[0, 2] + vc[0, 3])
-    fin_copies += everyone(total, vc.at[1], 2, zh, lambda d: at(go(zh, d), x, y))
+    fin_copies += everyone(
+        total, vc.at[1], 2, zh, lambda d: at(go(zh, d), x, y), (tiles.values(), y_copies.values(), z_copies.values())
+    )
     total = (vc[1, 0] + vc[1, 1]) + (vc[1, 2] + vc[1, 3])
     fin_copies += everyone(total, vd, 3, y, lambda d: at(zh, x, go(y, d)))
     for k in range(N):
         out_ref[pl.ds(k * piece, piece), :] = vd[k]
-
-    for group in (slab_p.values(), slab_f.values(), tiles.values(), y_copies.values(), z_copies.values(), fin_copies):
-        for cp in group:
-            cp.wait_send()
+    out_ref[pl.ds(AW, 8), :] = jnp.concatenate([vd[0][0:8, AW:]] * 4, axis=1)
+    for cp in fin_copies:
+        cp.wait_send()
 
 
 def shards(three_index, occ_energy, vir_energy):
@@ -311,7 +346,7 @@
     dma = pltpu.SemaphoreType.DMA
     out = pl.pallas_call(
         kernel,
-        out_shape=jax.ShapeDtypeStruct((AW, LANE), F32),
+        out_shape=jax.ShapeDtypeStruct((AW + 8, LANE), F32),
         in_specs=[
             pl.BlockSpec(memory_space=pl.ANY),
             pl.BlockSpec(memory_space=pltpu.SMEM),
@@ -324,9 +359,9 @@
             pltpu.VMEM((2, N * depth * occ, WIDE), bf16),
             pltpu.VMEM((CHUNKS, N, per, WIDE), LINK),
             pltpu.VMEM((CHUNKS, 3, per, WIDE), LINK),
-            pltpu.VMEM((CHUNKS, N, fin, WIDE), LINK),
-            pltpu.VMEM((CHUNKS, N, fin, OPW), LINK),
-            pltpu.VMEM((CHUNKS, N, fin, RESTW), LINK),
+            pltpu.VMEM((CHUNKS // 2, N, 2, fin, WIDE), LINK),
+            pltpu.VMEM((CHUNKS // 2, N, 2, fin, OPW), LINK),
+            pltpu.VMEM((CHUNKS // 2, 3, 2, fin, RESTW), LINK),
             pltpu.VMEM((CHUNKS * fin, WIDE), F32),
             pltpu.VMEM((AW, LANE), F32),
             pltpu.VMEM((3, piece, LANE), F32),
@@ -336,16 +371,17 @@
             dma((CHUNKS, N)), dma((CHUNKS, N)),
             dma((3, 7)), dma((3, 7)),
             dma((CHUNKS, 3)), dma((CHUNKS, 3)),
-            dma((CHUNKS, N)), dma((CHUNKS, N)),
-            dma((CHUNKS, N)), dma((CHUNKS, N)),
+            dma((CHUNKS // 2, N)), dma((CHUNKS // 2, N)),
+            dma((CHUNKS // 2, N)), dma((CHUNKS // 2, N)),
             dma((4, N)), dma((4, N)),
+            pltpu.SemaphoreType.REGULAR,
         ],
         compiler_params=pltpu.CompilerParams(
             collective_id=0, has_side_effects=True, vmem_limit_bytes=56 * 1024 * 1024
         ),
         cost_estimate=pl.CostEstimate(flops=4_000_000_000, bytes_accessed=8_000_000, transcendentals=0),
     )(view, occ_energy, vir_energy.reshape(vir // LANE, LANE))
-    return out[:, :AW], out[0, AW:AW + 4].reshape(2, 2)
+    return out[:AW, :AW], out[AW:AW + 2, :2]
 
 
 def solution(mesh):

time: 97.7 us -> 90.6 us (0.927)
  the two profiles are of different devices: /device:TPU:32 before, /device:TPU:2 now
where the time goes in v3:
time: 90.6 us; the launch traced here: 90.4 us
  Pallas kernels  87.1 us (96%)
  local copies, waits for them, and re-layouts  2.66 us (3%)
    pallas_call x1, Pallas kernels, shards(): pl.pallas_call(kernel, out_shape=jax.ShapeDtypeStruct((AW + 8, LANE), F32...  87.1 us
    slice x2, local copies, waits for them, and re-layouts, shards(): return (out[:AW, :AW], out[AW:AW + 2, :2])  2.66 us

profile of v3, /device:TPU:2, one launch (start us, length us, event | category | flops | bytes accessed | tf_op | source)
XLA Modules:
  0.0 90.4 jit_solution(1101874954512359190)
XLA Ops:
  0.6 87.1 %shard_map.50 = f32[104,128]{1,0:T(8,128)} custom-call(bf16[200,32,2,128]{3,2,1,0:T(2,128)(2,1)} %bitcast.4, f32[16]{0:T(128)} %occ_ref.1, f32[32,128]{1,0:T(8,128)} %bitcast.5), custom_call_target="tpu_custom_call" | custom-call | flops 4000000000 | bytes 8000000 | tf_op jit(solution)/shard_map/pallas_call | solution.py:347
  87.7 1.2 %slice.7 = f32[2,2]{1,0:T(2,128)} slice(f32[104,128]{1,0:T(8,128)} %shard_map.50), slice={[96:98], [0:2]} | slice | bytes 32 | tf_op jit(solution)/shard_map/slice | solution.py:384
  88.9 1.4 %slice.6 = f32[96,96]{1,0:T(8,128)} slice(f32[104,128]{1,0:T(8,128)} %shard_map.50), slice={[0:96], [0:96]} | slice | bytes 73728 | tf_op jit(solution)/shard_map/slice | solution.py:384

commit v4 on v3

--- a/solution.py
+++ b/solution.py
@@ -226,6 +226,53 @@
         for c in chunks:
             multiply(c)
 
+    lane = lax.broadcasted_iota(jnp.int32, (fin, LANE), 1)
+    row = lax.broadcasted_iota(jnp.int32, (fin, LANE), 0)
+    ea = vir_ref[0:1, 0:AW]
+    eo = [occ_ref[2 * g], occ_ref[2 * g + 1]]
+    ep = [occ_ref[2 * prv], occ_ref[2 * prv + 1]]
+
+    def inner(a, b):
+        return jnp.sum(jnp.sum(a * b, axis=1, keepdims=True), axis=0, keepdims=True)
+
+    def densities(start, stop):
+        columns = []
+        for c in range(start, stop):
+            lt = c * N + place[c % 2]
+            offset = place[1 - c % 2] * per + zh * fin
+            line = jnp.broadcast_to(vir_ref[pl.ds(lt, 1), :], (fin, LANE))
+            columns.append(jnp.sum(jnp.where(lane == row + offset, line, 0.0), axis=1, keepdims=True))
+        eb = jnp.concatenate(columns, axis=0)
+
+        def amplitude(k, ei, ej):
+            return tb[start * fin:stop * fin, k * AW:(k + 1) * AW] / (((ei + ej) - ea) - eb)
+
+        op = [[amplitude(2 * i + j, eo[i], ep[j]) for j in range(2)] for i in range(2)]
+        po = [[amplitude(4 + 2 * i + j, ep[i], eo[j]) for j in range(2)] for i in range(2)]
+        ow = [amplitude(8, eo[0], eo[1]), amplitude(9, eo[1], eo[0])]
+        mop = [[2.0 * op[i][j] - po[j][i] for j in range(2)] for i in range(2)]
+        mpo = [[2.0 * po[i][j] - op[j][i] for j in range(2)] for i in range(2)]
+        mow = [2.0 * ow[0] - ow[1], 2.0 * ow[1] - ow[0]]
+        left = jnp.concatenate(op[0] + op[1] + po[0] + po[1] + ow, axis=0)
+        right = jnp.concatenate(mop[0] + mop[1] + mpo[0] + mpo[1] + mow, axis=0)
+        vv = lax.dot_general(
+            left, right, (((0,), (0,)), ((), ())), preferred_element_type=F32, precision=lax.Precision.HIGHEST
+        )
+        oo = []
+        for i in range(2):
+            for j in range(2):
+                s = inner(op[i][0], mop[j][0]) + inner(op[i][1], mop[j][1])
+                if i == j:
+                    s = s + inner(ow[i], mow[i])
+                oo.append(s)
+        corner = jnp.zeros((AW, LANE - AW), F32)
+        cl = lax.broadcasted_iota(jnp.int32, corner.shape, 1)
+        cr = lax.broadcasted_iota(jnp.int32, corner.shape, 0)
+        for k in range(4):
+            here = jnp.logical_and(cr == k // 2, cl == k % 2)
+            corner = jnp.where(here, jnp.broadcast_to(oo[k], corner.shape), corner)
+        return jnp.concatenate([vv, corner], axis=1)
+
     multiply_all(0, 1, 2, 3)
     multiply_all(4, 5)
     exchange(6, 7)
@@ -236,59 +283,16 @@
 
     reduce_y(0)
     reduce_y(1)
+    reduce_y(2)
     multiply_all(6, 7)
-    reduce_y(2)
+    reduce_y(3)
     reduce_z(0)
     reduce_z(1)
-    reduce_y(3)
     reduce_z(2)
+    va[...] = densities(0, 6)
     reduce_z(3)
-
-    lane = lax.broadcasted_iota(jnp.int32, (fin, LANE), 1)
-    row = lax.broadcasted_iota(jnp.int32, (fin, LANE), 0)
-    columns = []
-    for c in range(CHUNKS):
-        lt = c * N + place[c % 2]
-        offset = place[1 - c % 2] * per + zh * fin
-        line = jnp.broadcast_to(vir_ref[pl.ds(lt, 1), :], (fin, LANE))
-        columns.append(jnp.sum(jnp.where(lane == row + offset, line, 0.0), axis=1, keepdims=True))
-    eb = jnp.concatenate(columns, axis=0)
-    ea = vir_ref[0:1, 0:AW]
-    eo = [occ_ref[2 * g], occ_ref[2 * g + 1]]
-    ep = [occ_ref[2 * prv], occ_ref[2 * prv + 1]]
-
-    def amplitude(k, ei, ej):
-        return tb[:, k * AW:(k + 1) * AW] / (((ei + ej) - ea) - eb)
-
-    op = [[amplitude(2 * i + j, eo[i], ep[j]) for j in range(2)] for i in range(2)]
-    po = [[amplitude(4 + 2 * i + j, ep[i], eo[j]) for j in range(2)] for i in range(2)]
-    ow = [amplitude(8, eo[0], eo[1]), amplitude(9, eo[1], eo[0])]
-    mop = [[2.0 * op[i][j] - po[j][i] for j in range(2)] for i in range(2)]
-    mpo = [[2.0 * po[i][j] - op[j][i] for j in range(2)] for i in range(2)]
-    mow = [2.0 * ow[0] - ow[1], 2.0 * ow[1] - ow[0]]
-    left = jnp.concatenate(op[0] + op[1] + po[0] + po[1] + ow, axis=0)
-    right = jnp.concatenate(mop[0] + mop[1] + mpo[0] + mpo[1] + mow, axis=0)
-    vv = lax.dot_general(
-        left, right, (((0,), (0,)), ((), ())), preferred_element_type=F32, precision=lax.Precision.HIGHEST
-    )
-
-    def inner(a, b):
-        return jnp.sum(jnp.sum(a * b, axis=1, keepdims=True), axis=0, keepdims=True)
-
-    oo = []
-    for i in range(2):
-        for j in range(2):
-            s = inner(op[i][0], mop[j][0]) + inner(op[i][1], mop[j][1])
-            if i == j:
-                s = s + inner(ow[i], mow[i])
-            oo.append(s)
-    corner = jnp.zeros((AW, LANE - AW), F32)
-    cl = lax.broadcasted_iota(jnp.int32, corner.shape, 1)
-    cr = lax.broadcasted_iota(jnp.int32, corner.shape, 0)
-    for k in range(4):
-        here = jnp.logical_and(cr == k // 2, cl == k % 2)
-        corner = jnp.where(here, jnp.broadcast_to(oo[k], corner.shape), corner)
-    va[...] = jnp.concatenate([2.0 * vv, -2.0 * corner], axis=1)
+    va[...] += densities(6, 8)
+
 
     piece = AW // N
     fin_copies = []
@@ -381,7 +385,7 @@
         ),
         cost_estimate=pl.CostEstimate(flops=4_000_000_000, bytes_accessed=8_000_000, transcendentals=0),
     )(view, occ_energy, vir_energy.reshape(vir // LANE, LANE))
-    return out[:AW, :AW], out[AW:AW + 2, :2]
+    return 2.0 * out[:AW, :AW], -2.0 * out[AW:AW + 2, :2]
 
 
 def solution(mesh):

time: 90.6 us -> 88.5 us (0.977)
  other arithmetic: 0 us -> 2.67 us
  local copies, waits for them, and re-layouts: 2.66 us -> 0 us
  Pallas kernels: 87.1 us -> 85 us
    mul x0 -> x2, other arithmetic: none -> 2.67 us  [shards(): return (2.0 * out[:AW, :AW], -2.0 * out[AW:AW + 2, :2])]
    slice x2 -> x0, local copies, waits for them, and re-layouts: 2.66 us -> none  [shards(): return (out[:AW, :AW], out[AW:AW + 2, :2])]
    pallas_call x1, Pallas kernels: 87.1 us -> 85 us  [shards(): pl.pallas_call(kernel, out_shape=jax.ShapeDtypeStruct((AW + 8, LANE), F32...]
where the time goes in v4:
time: 88.5 us; the launch traced here: 88.3 us
  Pallas kernels  85 us (96%)
  other arithmetic  2.67 us (3%)
    pallas_call x1, Pallas kernels, shards(): pl.pallas_call(kernel, out_shape=jax.ShapeDtypeStruct((AW + 8, LANE), F32...  85 us
    mul x2, other arithmetic, shards(): return (2.0 * out[:AW, :AW], -2.0 * out[AW:AW + 2, :2])  2.67 us

profile of v4, /device:TPU:2, one launch (start us, length us, event | category | flops | bytes accessed | tf_op | source)
XLA Modules:
  0.0 88.3 jit_solution(2794787871924233442)
XLA Ops:
  0.6 85.0 %shard_map.50 = f32[104,128]{1,0:T(8,128)} custom-call(bf16[200,32,2,128]{3,2,1,0:T(2,128)(2,1)} %bitcast.4, f32[16]{0:T(128)} %occ_ref.1, f32[32,128]{1,0:T(8,128)} %bitcast.5), custom_call_target="tpu_custom_call" | custom-call | flops 4000000000 | bytes 8000000 | tf_op jit(solution)/shard_map/pallas_call | solution.py:351
  85.6 1.2 %slice_multiply_fusion.1 = f32[2,2]{1,0:T(2,128)} fusion(f32[104,128]{1,0:T(8,128)} %shard_map.50), kind=kLoop, calls=%fused_computation.1 | loop fusion | flops 4 | bytes 32 | tf_op jit(solution)/shard_map/mul | solution.py:388
  86.9 1.4 %slice_multiply_fusion = f32[96,96]{1,0:T(8,128)} fusion(f32[104,128]{1,0:T(8,128)} %shard_map.50), kind=kLoop, calls=%fused_computation | loop fusion | flops 9216 | bytes 73728 | tf_op jit(solution)/shard_map/mul | solution.py:388

commit v5 on v4

--- a/solution.py
+++ b/solution.py
@@ -139,9 +139,10 @@
             locals_[c] = cp
 
     exchange(0, 1)
-    gather(2, 0)
-    gather(1, blocks - 1)
     for k in (1, 4, 3, 6, 2, 5):
+        if k == 2:
+            gather(2, 0)
+            gather(1, blocks - 1)
         slab_p[k].wait_recv()
         forward(sl.at[0, k], k)
     exchange(2, 3, 4, 5)
@@ -197,20 +198,26 @@
                 total = total + yb[c, d].astype(F32)
             for k in range(N):
                 sb[pair, k, c % 2] = total[k * fin:(k + 1) * fin].astype(LINK)
+            if pair == CHUNKS // 2 - 1:
+                send_z(pair, pair + c % 2, c % 2)
+        if pair < CHUNKS // 2 - 1:
+            send_z(pair, pair, slice(None))
+
+    def send_z(pair, sem, j):
         for d in (2, 1, 3, 0):
             zz = go(zh, d)
-            src = sb.at[pair, zz, :, :, pl.ds(0, OPW)]
-            cp = remote(src, zop.at[pair, d], os_.at[pair, d], or_.at[pair, d], at(zz, x, y, nxt))
+            src = sb.at[pair, zz, j, :, pl.ds(0, OPW)]
+            cp = remote(src, zop.at[pair, d, j], os_.at[sem, d], or_.at[sem, d], at(zz, x, y, nxt))
             cp.start()
-            z_copies[pair, d, 0] = cp
+            z_copies[pair, sem, d, 0] = cp
             if d:
-                src = sb.at[pair, zz, :, :, pl.ds(OPW, RESTW)]
-                cp = remote(src, zrest.at[pair, d - 1], rs.at[pair, d], rr.at[pair, d], at(zz, x, y))
+                src = sb.at[pair, zz, j, :, pl.ds(OPW, RESTW)]
+                cp = remote(src, zrest.at[pair, d - 1, j], rs.at[sem, d], rr.at[sem, d], at(zz, x, y))
                 cp.start()
-                z_copies[pair, d, 1] = cp
+                z_copies[pair, sem, d, 1] = cp
 
     def reduce_z(pair):
-        for cp in [z_copies[pair, d, j] for d in (0, 1, 3, 2) for j in (0, 1) if d or not j]:
+        for cp in [cp for key, cp in z_copies.items() if key[0] == pair]:
             cp.wait_recv()
         for j in (0, 1):
             first = zop[pair, 0, j].astype(F32)
@@ -375,8 +382,8 @@
             dma((CHUNKS, N)), dma((CHUNKS, N)),
             dma((3, 7)), dma((3, 7)),
             dma((CHUNKS, 3)), dma((CHUNKS, 3)),
-            dma((CHUNKS // 2, N)), dma((CHUNKS // 2, N)),
-            dma((CHUNKS // 2, N)), dma((CHUNKS // 2, N)),
+            dma((CHUNKS // 2 + 1, N)), dma((CHUNKS // 2 + 1, N)),
+            dma((CHUNKS // 2 + 1, N)), dma((CHUNKS // 2 + 1, N)),
             dma((4, N)), dma((4, N)),
             pltpu.SemaphoreType.REGULAR,
         ],

time: 88.5 us -> 89 us (level)
  no operation moved by 1% of the time
where the time goes in v5:
time: 89 us; the launch traced here: 88.7 us
  Pallas kernels  85.4 us (96%)
  other arithmetic  2.67 us (3%)
    pallas_call x1, Pallas kernels, shards(): pl.pallas_call(kernel, out_shape=jax.ShapeDtypeStruct((AW + 8, LANE), F32...  85.4 us
    mul x2, other arithmetic, shards(): return (2.0 * out[:AW, :AW], -2.0 * out[AW:AW + 2, :2])  2.67 us

profile of v5, /device:TPU:2, one launch (start us, length us, event | category | flops | bytes accessed | tf_op | source)
XLA Modules:
  0.0 88.7 jit_solution(7713772907352527849)
XLA Ops:
  0.6 85.4 %shard_map.50 = f32[104,128]{1,0:T(8,128)} custom-call(bf16[200,32,2,128]{3,2,1,0:T(2,128)(2,1)} %bitcast.4, f32[16]{0:T(128)} %occ_ref.1, f32[32,128]{1,0:T(8,128)} %bitcast.5), custom_call_target="tpu_custom_call" | custom-call | flops 4000000000 | bytes 8000000 | tf_op jit(solution)/shard_map/pallas_call | solution.py:358
  86.0 1.2 %slice_multiply_fusion.1 = f32[2,2]{1,0:T(2,128)} fusion(f32[104,128]{1,0:T(8,128)} %shard_map.50), kind=kLoop, calls=%fused_computation.1 | loop fusion | flops 4 | bytes 32 | tf_op jit(solution)/shard_map/mul | solution.py:395
  87.3 1.4 %slice_multiply_fusion = f32[96,96]{1,0:T(8,128)} fusion(f32[104,128]{1,0:T(8,128)} %shard_map.50), kind=kLoop, calls=%fused_computation | loop fusion | flops 9216 | bytes 73728 | tf_op jit(solution)/shard_map/mul | solution.py:395
